TPU v7x, 128 devices: a whole 4x4x4 slice. The times are simulated.
128 devices in a mesh: dp: 4 (over z_hi, core), seq: 32 (over y, z_lo, x).
Axes of the slice: x: 4, y: 4, z: 4 (z_hi: 2, z_lo: 2; z = z_hi * 2 + z_lo), core: 2. Of those that a mesh axis runs over, the one named last changes fastest.
Arguments:
- q_space: bfloat16 [128, 512, 2048], P(('dp', 'seq')), parts along dimension 0, may hold values from -6 to 6
- k_space: bfloat16 [128, 512, 2048], P(('dp', 'seq')), parts along dimension 0, may hold values from -6 to 6
- v_space: bfloat16 [128, 512, 2048], P(('dp', 'seq')), parts along dimension 0, may hold values from -6 to 6
- q_time: bfloat16 [128, 512, 2048], P(('dp', 'seq')), parts along dimension 0, may hold values from -6 to 6
- k_time: bfloat16 [128, 512, 2048], P(('dp', 'seq')), parts along dimension 0, may hold values from -6 to 6
- grad_out: bfloat16 [128, 512, 2048], P(('dp', 'seq')), parts along dimension 0, may hold values from -6 to 6
Outputs:
- grad_q_space: bfloat16 [128, 512, 2048], P(('dp', 'seq')), parts along dimension 0
- grad_k_space: bfloat16 [128, 512, 2048], P(('dp', 'seq')), parts along dimension 0
- grad_v_space: bfloat16 [128, 512, 2048], P(('dp', 'seq')), parts along dimension 0
- grad_q_time: bfloat16 [128, 512, 2048], P(('dp', 'seq')), parts along dimension 0
- grad_k_time: bfloat16 [128, 512, 2048], P(('dp', 'seq')), parts along dimension 0
There are 4 independent parts, one for each index of `dp`. A program takes and returns all parts, laid end to end along the dimension named above; each array names one. Nothing has to cross between parts.
All inputs are finite; a program needn't handle non-finite values.
Results may differ from a plain program's by a relative error of at most 0.0092.
Values may be sent and summed in bfloat16 or wider, within the bound.
A program may use at most 192 MiB of HBM per device.

v0:
```python
import jax
import jax.numpy as jnp
from jax import lax
from jax.sharding import PartitionSpec as P

HEADS = 16
HEAD_DIM = 128


def space_major(tensor):
    return tensor.reshape(tensor.shape[:-1] + (HEADS, HEAD_DIM)).transpose(0, 2, 1, 3)


def space_flat(tensor):
    return tensor.transpose(0, 2, 1, 3).reshape(tensor.shape[0], tensor.shape[2], HEADS * HEAD_DIM)


def time_major(tensor):
    return tensor.reshape(tensor.shape[:-1] + (HEADS, HEAD_DIM)).transpose(1, 2, 0, 3)


def time_flat(tensor):
    return tensor.transpose(2, 0, 1, 3).reshape(tensor.shape[2], tensor.shape[0], HEADS * HEAD_DIM)


def product(form, left, right):
    return jnp.einsum(form, left, right, preferred_element_type=jnp.float32)


def probabilities(queries, key_rows):
    scores = product("bhqd,bhkd->bhqk", queries, key_rows) * HEAD_DIM ** (-0.5)
    weights = jax.nn.softmax(scores, axis=-1)
    return (weights, weights.astype(jnp.bfloat16))


def attend_backward(queries, key_rows, values, weights, rounded, upstream):
    weight_grads = product("bhqd,bhkd->bhqk", upstream, values)
    value_grads = product("bhqk,bhqd->bhkd", rounded, upstream).astype(jnp.bfloat16)
    score_grads = weights * (weight_grads - jnp.sum(weights * weight_grads, axis=-1, keepdims=True))
    score_grads = score_grads.astype(jnp.bfloat16)
    query_grads = (product("bhqk,bhkd->bhqd", score_grads, key_rows) * HEAD_DIM ** (-0.5)).astype(
        jnp.bfloat16
    )
    key_grads = (product("bhqk,bhqd->bhkd", score_grads, queries) * HEAD_DIM ** (-0.5)).astype(
        jnp.bfloat16
    )
    return (query_grads, key_grads, value_grads)


def space_backward(space_query, space_keys, space_values, space_weights, space_rounded, grad_space):
    grads = attend_backward(
        space_query, space_keys, space_values, space_weights, space_rounded, space_major(grad_space)
    )
    return tuple((space_flat(entry) for entry in grads))


def shards(q_space, k_space, v_space, q_time, k_time, grad_out):
    space_query = space_major(q_space)
    space_keys = space_major(k_space)
    space_values = space_major(v_space)
    space_weights, space_rounded = probabilities(space_query, space_keys)
    space_out = space_flat(
        product("bhqk,bhkd->bhqd", space_rounded, space_values).astype(jnp.bfloat16)
    )
    time_query, time_keys, time_upstream, time_values = (
        lax.all_to_all(q_time, "seq", split_axis=1, concat_axis=0, tiled=True),
        lax.all_to_all(k_time, "seq", split_axis=1, concat_axis=0, tiled=True),
        lax.all_to_all(grad_out, "seq", split_axis=1, concat_axis=0, tiled=True),
        lax.all_to_all(space_out, "seq", split_axis=1, concat_axis=0, tiled=True),
    )
    time_query = time_major(time_query)
    time_keys = time_major(time_keys)
    time_weights, time_rounded = probabilities(time_query, time_keys)
    query_moved, keys_moved, space_moved = attend_backward(
        time_query,
        time_keys,
        time_major(time_values),
        time_weights,
        time_rounded,
        time_major(time_upstream),
    )
    query_moved = time_flat(query_moved)
    keys_moved = time_flat(keys_moved)
    space_moved = time_flat(space_moved)
    grad_q_time, grad_k_time, grad_space = (
        lax.all_to_all(query_moved, "seq", split_axis=0, concat_axis=1, tiled=True),
        lax.all_to_all(keys_moved, "seq", split_axis=0, concat_axis=1, tiled=True),
        lax.all_to_all(space_moved, "seq", split_axis=0, concat_axis=1, tiled=True),
    )
    grad_q_space, grad_k_space, grad_v_space = space_backward(
        space_query, space_keys, space_values, space_weights, space_rounded, grad_space
    )
    return (grad_q_space, grad_k_space, grad_v_space, grad_q_time, grad_k_time)


def solution(mesh):
    in_specs = (
        P(("dp", "seq"), None, None),
        P(("dp", "seq"), None, None),
        P(("dp", "seq"), None, None),
        P(("dp", "seq"), None, None),
        P(("dp", "seq"), None, None),
        P(("dp", "seq"), None, None),
    )
    out_specs = (
        P(("dp", "seq"), None, None),
        P(("dp", "seq"), None, None),
        P(("dp", "seq"), None, None),
        P(("dp", "seq"), None, None),
        P(("dp", "seq"), None, None),
    )
    return jax.shard_map(shards, mesh=mesh, in_specs=in_specs, out_specs=out_specs, check_vma=False)
```

profile of v0, /device:TPU:0, one launch (start us, length us, event | category | flops | bytes accessed | tf_op | source)
XLA Modules:
  0.0 396.2 jit_solution(2994544509177819420)
XLA Ops:
  0.6 6.8 %copy.147 = bf16[1,512,2048]{2,0,1:T(2,128)(2,1)} copy(bf16[1,512,2048]{2,1,0:T(8,128)(2,1)} %param.9) | data formatting | bytes 4194304 | tf_op args[3]
  7.9 13.1 %reduce.16 = bf16[512,2048]{1,0:T(8,128)(2,1)S(1)} reduce(bf16[512,1,2048]{2,1,0:T(2,128)(2,1)} %bitcast.147, bf16[]{:T(256)} %broadcast.40), dimensions={1}, to_apply=%bitcast.141.reduce_sub_computation | reduce | bytes 4194306
  20.9 2.8 reshape.171
  23.7 9.0 %all-to-all-start = ((bf16[32,2,16384]{2,1,0:T(2,128)(2,1)}), bf16[32,2,16384]{2,1,0:T(2,128)(2,1)S(1)}, u32[]{:S(2)}, u32[]{:S(2)}) async-start(bf16[32,2,16384]{2,1,0:T(2,128)(2,1)} %reshape.171), calls=%async_computation | async-start | bytes 4194304 | tf_op jit(solution)/shard_map/all_to_all | solution.py:66
  32.7 6.8 %copy.146 = bf16[1,512,2048]{2,0,1:T(2,128)(2,1)} copy(bf16[1,512,2048]{2,1,0:T(8,128)(2,1)} %param.10) | data formatting | bytes 4194304 | tf_op args[4]
  39.4 14.4 %reduce.15 = bf16[512,2048]{1,0:T(8,128)(2,1)} reduce(bf16[512,1,2048]{2,1,0:T(2,128)(2,1)} %bitcast.149, bf16[]{:T(256)} %broadcast.40), dimensions={1}, to_apply=%bitcast.140.reduce_sub_computation | reduce | bytes 4194306
  53.8 4.5 %reshape.169 = bf16[32,2,16384]{2,1,0:T(2,128)(2,1)} reshape(bf16[512,2048]{1,0:T(8,128)(2,1)} %reduce.15) | data formatting | bytes 4194304
  58.3 2.3 all-to-all-done
  60.6 1.4 copy-done.8
  62.0 6.5 %all-to-all-start.1 = ((bf16[32,2,16384]{2,1,0:T(2,128)(2,1)}), bf16[32,2,16384]{2,1,0:T(2,128)(2,1)}, u32[]{:S(2)}, u32[]{:S(2)}) async-start(bf16[32,2,16384]{2,1,0:T(2,128)(2,1)} %reshape.169), calls=%async_computation.1 | async-start | bytes 4194304 | tf_op jit(solution)/shard_map/all_to_all | solution.py:67
  68.5 3.9 copy.86
  72.4 2.9 copy.87
  75.3 4.6 %copy.88 = bf16[1,512,2048]{1,2,0:T(8,128)(2,1)} copy(bf16[1,512,2048]{2,1,0:T(8,128)(2,1)} %param.8) | data formatting | bytes 4194304 | tf_op jit(solution)/shard_map/reshape | solution.py:11
  79.9 6.7 %copy.145 = bf16[1,512,2048]{2,0,1:T(2,128)(2,1)} copy(bf16[1,512,2048]{2,1,0:T(8,128)(2,1)} %param.11) | data formatting | bytes 4194304 | tf_op args[5]
  86.6 14.4 %reduce.14 = bf16[512,2048]{1,0:T(8,128)(2,1)} reduce(bf16[512,1,2048]{2,1,0:T(2,128)(2,1)} %bitcast.150, bf16[]{:T(256)} %broadcast.40), dimensions={1}, to_apply=%bitcast.139.reduce_sub_computation | reduce | bytes 4194306
  101.0 4.5 %reshape.167 = bf16[32,2,16384]{2,1,0:T(2,128)(2,1)} reshape(bf16[512,2048]{1,0:T(8,128)(2,1)} %reduce.14) | data formatting | bytes 4194304
  105.5 10.1 %fusion.62 = (f32[16,512]{1,0:T(8,128)S(1)}, f32[16,512,512]{1,2,0:T(8,128)}) fusion(bf16[16,512,128]{1,2,0:T(8,128)(2,1)} %bitcast.162, bf16[16,512,128]{1,2,0:T(8,128)(2,1)S(1)} %bitcast.151), kind=kOutput, calls=%fused_computation.59 | convolution fusion | flops 1086325248 | bytes 21004288 | tf_op jit(solution)/shard_map/sub | solution.py:32
  115.6 9.0 %all-to-all-start.2 = ((bf16[32,2,16384]{2,1,0:T(2,128)(2,1)}), bf16[32,2,16384]{2,1,0:T(2,128)(2,1)}, u32[]{:S(2)}, u32[]{:S(2)}) async-start(bf16[32,2,16384]{2,1,0:T(2,128)(2,1)} %reshape.167), calls=%async_computation.2 | async-start | bytes 4194304 | tf_op jit(solution)/shard_map/all_to_all | solution.py:68
  124.6 7.7 %fusion.44 = bf16[16,512,128]{1,2,0:T(8,128)(2,1)S(1)} fusion(bf16[16,512,128]{1,2,0:T(8,128)(2,1)} %bitcast.164, f32[16,512,512]{1,2,0:T(8,128)} %get-tuple-element.23, f32[16,512]{1,0:T(8,128)S(1)} %get-tuple-element.22), kind=kOutput, calls=%fused_computation.46 | convolution fusion | flops 1083179008 | bytes 21004288 | tf_op jit(solution)/shard_map/bhqk,bhkd->bhqd/dot_general | solution.py:27
  132.3 7.7 %copy.69 = bf16[1,512,2048]{2,0,1:T(2,128)(2,1)} copy(bf16[1,512,2048]{1,2,0:T(8,128)(2,1)S(1)} %bitcast.161) | data formatting | bytes 4194304 | tf_op jit(solution)/shard_map/reshape | solution.py:15
  140.0 14.4 %reduce.17 = bf16[512,2048]{1,0:T(8,128)(2,1)} reduce(bf16[512,1,2048]{2,1,0:T(2,128)(2,1)} %bitcast.148, bf16[]{:T(256)} %broadcast.40), dimensions={1}, to_apply=%bitcast.112.reduce_sub_computation | reduce | bytes 4194306
  154.4 4.7 %reshape.173 = bf16[32,2,16384]{2,1,0:T(2,128)(2,1)} reshape(bf16[512,2048]{1,0:T(8,128)(2,1)} %reduce.17) | data formatting | bytes 4194304
  159.0 6.8 %reshape.172 = bf16[512,1,2048]{2,1,0:T(2,128)(2,1)} reshape(bf16[32,2,16384]{2,1,0:T(2,128)(2,1)S(1)} %copy-done.9) | data formatting | bytes 4194304
  165.8 12.8 %bitcast_reduce_fusion.1 = bf16[512,2048]{1,0:T(8,128)(2,1)S(1)} fusion(bf16[512,1,2048]{2,1,0:T(2,128)(2,1)} %reshape.172), kind=kLoop, calls=%fused_computation.61 | loop fusion | bytes 4194304 | tf_op jit(solution)/shard_map/all_to_all | solution.py:66
  179.3 10.6 %reshape.170 = bf16[512,1,2048]{2,1,0:T(2,128)(2,1)} reshape(bf16[32,2,16384]{2,1,0:T(2,128)(2,1)} %all-to-all-done.1) | data formatting | bytes 4194304
  189.9 12.8 %bitcast_reduce_fusion.2 = bf16[512,2048]{1,0:T(8,128)(2,1)S(1)} fusion(bf16[512,1,2048]{2,1,0:T(2,128)(2,1)} %reshape.170), kind=kLoop, calls=%fused_computation.62 | loop fusion | bytes 4194304 | tf_op jit(solution)/shard_map/all_to_all | solution.py:67
  202.7 2.0 copy.92
  204.7 8.7 %all-to-all-start.4 = ((bf16[32,2,16384]{2,1,0:T(2,128)(2,1)}), bf16[32,2,16384]{2,1,0:T(2,128)(2,1)}, u32[]{:S(2)}, u32[]{:S(2)}) async-start(bf16[32,2,16384]{2,1,0:T(2,128)(2,1)} %reshape.173), calls=%async_computation.4 | async-start | bytes 4194304 | tf_op jit(solution)/shard_map/all_to_all | solution.py:69
  213.4 10.5 %reshape.168 = bf16[512,1,2048]{2,1,0:T(2,128)(2,1)} reshape(bf16[32,2,16384]{2,1,0:T(2,128)(2,1)} %all-to-all-done.2) | data formatting | bytes 4194304
  223.8 12.8 %bitcast_reduce_fusion.3 = bf16[512,2048]{1,0:T(8,128)(2,1)S(1)} fusion(bf16[512,1,2048]{2,1,0:T(2,128)(2,1)} %reshape.168), kind=kLoop, calls=%fused_computation.63 | loop fusion | bytes 4194304 | tf_op jit(solution)/shard_map/all_to_all | solution.py:68
  237.3 0.9 copy-done.1
  238.3 2.8 fusion.25
  241.0 9.5 %fusion.61 = (f32[16,16,32]{2,1,0:T(8,128)S(1)}, f32[16,16,32,32]{2,3,1,0:T(8,128)S(1)}) fusion(f32[16,16,32,32]{2,3,1,0:T(8,128)S(1)} %fusion.25), kind=kOutput, calls=%fused_computation.58 | output fusion | flops 1048607 | bytes 2129920 | tf_op jit(solution)/shard_map/sub | solution.py:32
  250.6 1.6 convert_bitcast_fusion
  252.5 0.8 copy.60
  253.3 2.3 reshape.151
  255.6 8.7 %all-to-all-start.3 = ((bf16[32,16,2048]{2,1,0:T(8,128)(2,1)}), bf16[32,16,2048]{2,1,0:T(8,128)(2,1)}, u32[]{:S(2)}, u32[]{:S(2)}) async-start(bf16[32,16,2048]{2,1,0:T(8,128)(2,1)} %reshape.151), calls=%async_computation.3 | async-start | bytes 4194304 | tf_op jit(solution)/shard_map/all_to_all | solution.py:88
  264.3 10.5 %reshape.174 = bf16[512,1,2048]{2,1,0:T(2,128)(2,1)} reshape(bf16[32,2,16384]{2,1,0:T(2,128)(2,1)} %all-to-all-done.4) | data formatting | bytes 4194304
  274.8 12.9 %bitcast_reduce_fusion = bf16[512,2048]{1,0:T(8,128)(2,1)S(1)} fusion(bf16[512,1,2048]{2,1,0:T(2,128)(2,1)} %reshape.174), kind=kLoop, calls=%fused_computation.60 | loop fusion | bytes 4194304 | tf_op jit(solution)/shard_map/all_to_all | solution.py:69
  287.7 0.6 copy.95
  288.4 1.5 copy-done.4
  289.9 3.5 fusion.6
  293.4 1.4 fusion.8
  295.0 1.8 fusion.53
  296.8 2.1 copy.72
  299.0 4.4 %reshape.161 = bf16[32,16,2048]{2,1,0:T(8,128)(2,1)} reshape(bf16[32,16,16,128]{3,2,1,0:T(8,128)(2,1)} %copy.72) | data formatting | bytes 4194304 | tf_op jit(solution)/shard_map/reshape | solution.py:23
  303.4 3.1 fusion.56
  306.5 0.8 copy.73
  307.3 2.3 reshape.162
  309.6 8.4 %all-to-all-start.6 = ((bf16[32,16,2048]{2,1,0:T(8,128)(2,1)}), bf16[32,16,2048]{2,1,0:T(8,128)(2,1)S(1)}, u32[]{:S(2)}, u32[]{:S(2)}) async-start(bf16[32,16,2048]{2,1,0:T(8,128)(2,1)} %reshape.162), calls=%async_computation.6 | async-start | bytes 4194304 | tf_op jit(solution)/shard_map/all_to_all | solution.py:87
  318.0 2.2 copy.94
  320.3 1.7 bitcast_bitcast_fusion
  322.5 10.7 %multiply_reduce_fusion = (f32[16,512]{1,0:T(8,128)S(1)}, f32[16,512,512]{1,2,0:T(8,128)}) fusion(f32[16,512,512]{1,2,0:T(8,128)} %get-tuple-element.23, f32[16,512]{1,0:T(8,128)S(1)} %get-tuple-element.22, bf16[16,512,128]{1,2,0:T(8,128)(2,1)S(1)} %bitcast.165, bf16[1,512,16,128]{3,2,1,0:T(8,128)(2,1)S(1)} %bitcast.160), kind=kOutput, calls=%fused_computation.3 | convolution fusion | flops 1086316544 | bytes 37814272 | tf_op jit(solution)/shard_map/bhqd,bhkd->bhqk/dot_general | solution.py:27
  333.2 15.1 %multiply_convert_fusion = bf16[16,512,512]{1,2,0:T(8,128)(2,1)} fusion(f32[16,512,512]{1,2,0:T(8,128)} %get-tuple-element.25, f32[16,512]{1,0:T(8,128)S(1)} %get-tuple-element.24, f32[16,512,512]{1,2,0:T(8,128)} %get-tuple-element.23, f32[16,512]{1,0:T(8,128)S(1)} %get-tuple-element.22), kind=kLoop, calls=%fused_computation.2 | loop fusion | flops 16777216 | bytes 42008576 | tf_op jit(solution)/shard_map/convert_element_type | solution.py:40
  348.2 1.3 copy-done.10
  349.6 8.4 %all-to-all-start.5 = ((bf16[32,16,2048]{2,1,0:T(8,128)(2,1)}), bf16[32,16,2048]{2,1,0:T(8,128)(2,1)}, u32[]{:S(2)}, u32[]{:S(2)}) async-start(bf16[32,16,2048]{2,1,0:T(8,128)(2,1)} %reshape.161), calls=%async_computation.5 | async-start | bytes 4194304 | tf_op jit(solution)/shard_map/all_to_all | solution.py:86
  358.0 8.9 %fusion.39 = bf16[16,512,128]{1,2,0:T(8,128)(2,1)} fusion(bf16[16,512,128]{2,0,1:T(8,128)(2,1)} %bitcast_bitcast_fusion, f32[16,512,512]{1,2,0:T(8,128)} %get-tuple-element.23, f32[16,512]{1,0:T(8,128)S(1)} %get-tuple-element.22), kind=kOutput, calls=%fused_computation.45 | convolution fusion | flops 1083179008 | bytes 21004288 | tf_op jit(solution)/shard_map/bhqk,bhqd->bhkd/dot_general | solution.py:27
  367.0 4.1 %copy.76 = bf16[1,512,2048]{2,1,0:T(8,128)(2,1)} copy(bf16[1,512,2048]{1,2,0:T(8,128)(2,1)} %bitcast.170) | data formatting | bytes 4194304
  371.0 6.1 %multiply_convert_fusion.4 = bf16[16,512,128]{1,2,0:T(8,128)(2,1)} fusion(bf16[16,512,128]{1,2,0:T(8,128)(2,1)S(1)} %bitcast.152, bf16[16,512,512]{1,2,0:T(8,128)(2,1)} %multiply_convert_fusion), kind=kOutput, calls=%fused_computation.21 | convolution fusion | flops 1075838976 | bytes 12582912 | tf_op jit(solution)/shard_map/bhqk,bhkd->bhqd/dot_general | solution.py:27
  377.2 7.7 %multiply_convert_fusion.3 = bf16[16,512,128]{1,2,0:T(8,128)(2,1)} fusion(bf16[16,512,512]{1,2,0:T(8,128)(2,1)} %multiply_convert_fusion, bf16[16,512,128]{1,2,0:T(8,128)(2,1)S(1)} %bitcast.163), kind=kOutput, calls=%fused_computation.20 | convolution fusion | flops 1075838976 | bytes 12582912 | tf_op jit(solution)/shard_map/bhqk,bhqd->bhkd/dot_general | solution.py:27
  384.8 2.4 copy.74
  387.2 3.9 copy.75
  391.1 3.3 copy.150
  394.4 1.3 copy.151
  (37 shorter events, 2.8 us)
Async XLA Ops:
  23.7 36.9 %all-to-all-start = ((bf16[32,2,16384]{2,1,0:T(2,128)(2,1)}), bf16[32,2,16384]{2,1,0:T(2,128)(2,1)S(1)}, u32[]{:S(2)}, u32[]{:S(2)}) async-start(bf16[32,2,16384]{2,1,0:T(2,128)(2,1)} %reshape.171), calls=%async_computation | async-start | bytes 4194304 | tf_op jit(solution)/shard_map/all_to_all | solution.py:66
  60.6 1.4 copy-start.8
  62.0 53.6 %all-to-all-start.1 = ((bf16[32,2,16384]{2,1,0:T(2,128)(2,1)}), bf16[32,2,16384]{2,1,0:T(2,128)(2,1)}, u32[]{:S(2)}, u32[]{:S(2)}) async-start(bf16[32,2,16384]{2,1,0:T(2,128)(2,1)} %reshape.169), calls=%async_computation.1 | async-start | bytes 4194304 | tf_op jit(solution)/shard_map/all_to_all | solution.py:67
  75.3 30.2 %copy-start.5 = (bf16[1,512,2048]{1,2,0:T(8,128)(2,1)}, bf16[1,512,2048]{1,2,0:T(8,128)(2,1)S(1)}, u32[]{:S(2)}) copy-start(bf16[1,512,2048]{1,2,0:T(8,128)(2,1)S(1)} %copy.87) | copy-start | bytes 6291460
  115.6 89.1 %all-to-all-start.2 = ((bf16[32,2,16384]{2,1,0:T(2,128)(2,1)}), bf16[32,2,16384]{2,1,0:T(2,128)(2,1)}, u32[]{:S(2)}, u32[]{:S(2)}) async-start(bf16[32,2,16384]{2,1,0:T(2,128)(2,1)} %reshape.167), calls=%async_computation.2 | async-start | bytes 4194304 | tf_op jit(solution)/shard_map/all_to_all | solution.py:68
  154.4 4.7 %copy-start.9 = (bf16[32,2,16384]{2,1,0:T(2,128)(2,1)S(1)}, bf16[32,2,16384]{2,1,0:T(2,128)(2,1)}, u32[]{:S(2)}) copy-start(bf16[32,2,16384]{2,1,0:T(2,128)(2,1)} %copy-done.8) | copy-start | bytes 6291460
  179.3 58.0 %copy-start = (bf16[64,8,16,128]{3,2,1,0:T(8,128)(2,1)}, bf16[64,8,16,128]{3,2,1,0:T(8,128)(2,1)S(1)}, u32[]{:S(2)}) copy-start(bf16[64,8,16,128]{3,2,1,0:T(8,128)(2,1)S(1)} %copy.91) | copy-start | bytes 6291460
  204.7 50.9 %all-to-all-start.4 = ((bf16[32,2,16384]{2,1,0:T(2,128)(2,1)}), bf16[32,2,16384]{2,1,0:T(2,128)(2,1)}, u32[]{:S(2)}, u32[]{:S(2)}) async-start(bf16[32,2,16384]{2,1,0:T(2,128)(2,1)} %reshape.173), calls=%async_computation.4 | async-start | bytes 4194304 | tf_op jit(solution)/shard_map/all_to_all | solution.py:69
  236.7 1.6 copy-start.1
  237.3 13.3 %copy-start.14 = (bf16[64,8,16,128]{3,2,1,0:T(8,128)(2,1)}, bf16[64,8,16,128]{3,2,1,0:T(8,128)(2,1)S(1)}, u32[]{:S(2)}) copy-start(bf16[64,8,16,128]{3,2,1,0:T(8,128)(2,1)S(1)} %copy.93) | copy-start | bytes 6291460
  250.5 1.9 copy-start.3
  255.6 54.1 %all-to-all-start.3 = ((bf16[32,16,2048]{2,1,0:T(8,128)(2,1)}), bf16[32,16,2048]{2,1,0:T(8,128)(2,1)}, u32[]{:S(2)}, u32[]{:S(2)}) async-start(bf16[32,16,2048]{2,1,0:T(8,128)(2,1)} %reshape.151), calls=%async_computation.3 | async-start | bytes 4194304 | tf_op jit(solution)/shard_map/all_to_all | solution.py:88
  274.8 13.6 %copy-start.15 = (bf16[64,8,16,128]{3,2,1,0:T(8,128)(2,1)S(1)}, bf16[64,8,16,128]{3,2,1,0:T(8,128)(2,1)}, u32[]{:S(2)}) copy-start(bf16[64,8,16,128]{3,2,1,0:T(8,128)(2,1)} %copy-done.14) | copy-start | bytes 6291460
  287.7 2.2 copy-start.4
  293.4 1.6 copy-start.2
  309.6 38.6 %all-to-all-start.6 = ((bf16[32,16,2048]{2,1,0:T(8,128)(2,1)}), bf16[32,16,2048]{2,1,0:T(8,128)(2,1)S(1)}, u32[]{:S(2)}, u32[]{:S(2)}) async-start(bf16[32,16,2048]{2,1,0:T(8,128)(2,1)} %reshape.162), calls=%async_computation.6 | async-start | bytes 4194304 | tf_op jit(solution)/shard_map/all_to_all | solution.py:87
  320.3 2.2 copy-start.13
  348.2 1.4 copy-start.10
  349.6 35.3 %all-to-all-start.5 = ((bf16[32,16,2048]{2,1,0:T(8,128)(2,1)}), bf16[32,16,2048]{2,1,0:T(8,128)(2,1)}, u32[]{:S(2)}, u32[]{:S(2)}) async-start(bf16[32,16,2048]{2,1,0:T(8,128)(2,1)} %reshape.161), calls=%async_computation.5 | async-start | bytes 4194304 | tf_op jit(solution)/shard_map/all_to_all | solution.py:86
  367.0 4.1 %copy-start.6 = (bf16[1,512,2048]{1,2,0:T(8,128)(2,1)S(1)}, bf16[1,512,2048]{1,2,0:T(8,128)(2,1)}, u32[]{:S(2)}) copy-start(bf16[1,512,2048]{1,2,0:T(8,128)(2,1)} %copy-done.5) | copy-start | bytes 6291460
  371.0 6.1 %copy-start.12 = (bf16[1,512,2048]{1,2,0:T(8,128)(2,1)S(1)}, bf16[1,512,2048]{1,2,0:T(8,128)(2,1)}, u32[]{:S(2)}) copy-start(bf16[1,512,2048]{1,2,0:T(8,128)(2,1)} %copy.86) | copy-start | bytes 6291460
  377.2 7.7 %copy-start.7 = (bf16[16,512,128]{1,2,0:T(8,128)(2,1)S(1)}, bf16[16,512,128]{1,2,0:T(8,128)(2,1)}, u32[]{:S(2)}) copy-start(bf16[16,512,128]{1,2,0:T(8,128)(2,1)} %multiply_convert_fusion.4) | copy-start | bytes 6291460
  391.1 3.3 copy-start.11
where the time goes:
time: 404 us; the launch traced here: 396 us
  local copies, waits for them, and re-layouts  188 us (47%)
  other arithmetic  82.1 us (20%)
  matrix products  64 us (16%)
  starting transfers between devices  58.7 us (15%)
    unnamed x54, local copies, waits for them, and re-layouts  103 us
    unnamed x4, other arithmetic  56.2 us
    dot_general x10, matrix products, product(): return jnp.einsum(form, left, right, preferred_element_type=jnp.float32)  53.9 us
    convert_element_type x2, other arithmetic, attend_backward(): score_grads = score_grads.astype(jnp.bfloat16)  16.5 us
    all_to_all x1, local copies, waits for them, and re-layouts, shards(): lax.all_to_all(space_out, 'seq', split_axis=1, concat_axis=0, tiled=True)  12.9 us
    all_to_all x1, local copies, waits for them, and re-layouts, shards(): lax.all_to_all(k_time, 'seq', split_axis=1, concat_axis=0, tiled=True)  12.8 us
    all_to_all x1, local copies, waits for them, and re-layouts, shards(): lax.all_to_all(q_time, 'seq', split_axis=1, concat_axis=0, tiled=True)  12.8 us
    all_to_all x1, local copies, waits for them, and re-layouts, shards(): lax.all_to_all(grad_out, 'seq', split_axis=1, concat_axis=0, tiled=True)  12.8 us
  transfers between devices with their start and end apart: 7, of which 1 were waited for; matrix products, arithmetic and copies ran while one was open for 74% of the time, Pallas kernels for 0%

commit v1 on v0

v1 whole, which is shorter than its diff:
```python
import functools
import math

import jax
import jax.numpy as jnp
from jax import lax
from jax.experimental import pallas as pl
from jax.experimental.pallas import tpu as pltpu
from jax.sharding import PartitionSpec as P

HEADS = 16
HEAD_DIM = 128
SCALE = HEAD_DIM**-0.5
SCALE2 = SCALE * math.log2(math.e)
MESH = pl.DeviceIdType.MESH

FRAMES = 32
POS = 512
OWN = POS // FRAMES
WIDTH = HEADS * HEAD_DIM
CHUNKS = 4
COLS = WIDTH // CHUNKS
CHUNK_HEADS = HEADS // CHUNKS


def product(left, right, contract):
    return lax.dot_general(left, right, (contract, ((), ())), preferred_element_type=jnp.float32)


def plain(left, right):
    return product(left, right, ((1,), (0,)))


def against(left, right):
    return product(left, right, ((1,), (1,)))


def probabilities(queries, key_rows, bias=None):
    scores = against(key_rows, queries) * SCALE2
    if bias is not None:
        scores = (scores.reshape(FRAMES, OWN, POS) + bias[None]).reshape(POS, POS)
    scores = jnp.exp2(scores - jnp.max(scores, axis=0, keepdims=True))
    return scores * (1.0 / jnp.sum(scores, axis=0, keepdims=True))


def backward(queries, key_rows, values, upstream, bias=None):
    weights = probabilities(queries, key_rows, bias)
    value_grads = plain(weights.astype(jnp.bfloat16), upstream)
    weight_grads = against(values, upstream)
    weighted = weights * weight_grads
    score_grads = weighted - weights * jnp.sum(weighted, axis=0, keepdims=True)
    score_grads = score_grads.astype(jnp.bfloat16)
    key_grads = plain(score_grads, queries) * SCALE
    query_grads = (plain(key_rows.T, score_grads) * SCALE).T
    return (
        query_grads.astype(jnp.bfloat16),
        key_grads.astype(jnp.bfloat16),
        value_grads.astype(jnp.bfloat16),
    )


def kernel(
    q_space, k_space, v_space, q_time, k_time, grad_out,
    gq_space, gk_space, gv_space, gq_time, gk_time,
    sq, sk, sv, so, gs, held, made, done, bias,
    load_sem, send_sem, qkg_sem, so_sem, gs_sem, back_sem, own_sem, store_sem,
):
    seq, dp = lax.axis_index("seq"), lax.axis_index("dp")
    my_rows = pl.ds(pl.multiple_of(seq * OWN, OWN), OWN)

    def columns(chunk):
        return pl.ds(pl.multiple_of(chunk * COLS, COLS), COLS)

    def head_columns(head):
        return pl.ds(pl.multiple_of(head * HEAD_DIM, HEAD_DIM), HEAD_DIM)

    def peer_of(step):
        y = lax.rem(seq // 8 + step // 8, 4)
        z = lax.rem(seq // 4 + step // 4, 2)
        x = lax.rem(seq + step, 4)
        return y * 8 + z * 4 + x

    def rows_of(device):
        return pl.ds(pl.multiple_of(device * OWN, OWN), OWN)

    def spread(chunk, moves):
        cols = columns(chunk)

        def one(step, carry):
            peer = peer_of(step)
            for source, target, sent, landed in moves:
                pltpu.make_async_remote_copy(
                    src_ref=source.at[rows_of(peer), cols],
                    dst_ref=target.at[my_rows, cols],
                    send_sem=sent,
                    recv_sem=landed,
                    device_id=(dp, peer),
                    device_id_type=MESH,
                ).start()
            return carry

        lax.fori_loop(1, FRAMES, one, 0)
        for source, target, sent, landed in moves:
            pltpu.make_async_copy(
                source.at[my_rows, cols], target.at[my_rows, cols], landed
            ).start()

    def wait_for(ref, sem):
        pltpu.make_async_copy(ref, ref, sem).wait()

    spatial = ((q_space, sq), (k_space, sk), (v_space, sv))
    for chunk in range(CHUNKS):
        cols = pl.ds(chunk * COLS, COLS)
        for at, (source, target) in enumerate(spatial):
            pltpu.make_async_copy(
                source.at[:, cols], target.at[:, cols], load_sem.at[at, chunk]
            ).start()

    def send_inputs(chunk, carry):
        spread(
            chunk,
            [
                (source, held.at[at], send_sem.at[at], qkg_sem.at[at, chunk])
                for at, source in enumerate((q_time, k_time, grad_out))
            ],
        )
        return carry

    lax.fori_loop(0, CHUNKS, send_inputs, 0)

    rows = lax.broadcasted_iota(jnp.int32, (OWN, POS), 0)
    lanes = lax.broadcasted_iota(jnp.int32, (OWN, POS), 1)
    bias[...] = jnp.where(rows == lanes % OWN, 0.0, -1e30).astype(jnp.float32)

    def space_forward(chunk, carry):
        cols = columns(chunk)
        for at, (source, target) in enumerate(spatial):
            wait_for(target.at[:, cols], load_sem.at[at, chunk])

        def one(index, carry):
            here = head_columns(chunk * CHUNK_HEADS + index)
            weights = probabilities(sq[:, here], sk[:, here]).astype(jnp.bfloat16)
            so[:, here] = plain(sv[:, here].T, weights).T.astype(jnp.bfloat16)
            return carry

        lax.fori_loop(0, CHUNK_HEADS, one, 0)
        spread(chunk, [(so, held.at[3], send_sem.at[3], so_sem.at[chunk])])
        return carry

    lax.fori_loop(0, CHUNKS, space_forward, 0)

    def time_core(chunk, carry):
        cols = columns(chunk)
        for at in range(3):
            wait_for(held.at[at, :, cols], qkg_sem.at[at, chunk])
        wait_for(held.at[3, :, cols], so_sem.at[chunk])

        def one(index, carry):
            here = head_columns(chunk * CHUNK_HEADS + index)
            query_grads, key_grads, value_grads = backward(
                held[0, :, here], held[1, :, here], held[3, :, here], held[2, :, here], bias[...]
            )
            made[0, :, here] = value_grads
            made[1, :, here] = query_grads
            made[2, :, here] = key_grads
            return carry

        lax.fori_loop(0, CHUNK_HEADS, one, 0)
        spread(chunk, [(made.at[0], gs, send_sem.at[4], gs_sem.at[chunk])])
        spread(
            chunk,
            [
                (made.at[1], gq_time, send_sem.at[5], back_sem.at[0]),
                (made.at[2], gk_time, send_sem.at[6], back_sem.at[1]),
            ],
        )
        return carry

    lax.fori_loop(0, CHUNKS, time_core, 0)

    outs = (gq_space, gk_space, gv_space)

    def space_back(chunk, carry):
        cols = columns(chunk)
        wait_for(gs.at[:, cols], gs_sem.at[chunk])

        def one(index, carry):
            here = head_columns(chunk * CHUNK_HEADS + index)
            grads = backward(sq[:, here], sk[:, here], sv[:, here], gs[:, here])
            for at in range(3):
                done[at, :, here] = grads[at]
            return carry

        lax.fori_loop(0, CHUNK_HEADS, one, 0)
        for at in range(3):
            pltpu.make_async_copy(
                done.at[at, :, cols], outs[at].at[:, cols], store_sem.at[at, chunk]
            ).start()
        return carry

    lax.fori_loop(0, CHUNKS, space_back, 0)

    sent = POS - OWN
    for at in range(7):
        wait_for(held.at[0, pl.ds(0, sent)], send_sem.at[at])
    wait_for(gq_time, back_sem.at[0])
    wait_for(gk_time, back_sem.at[1])

    def stored(chunk, carry):
        for at in range(3):
            pltpu.make_async_copy(
                done.at[at, :, columns(chunk)],
                outs[at].at[:, columns(chunk)],
                store_sem.at[at, chunk],
            ).wait()
        return carry

    lax.fori_loop(0, CHUNKS, stored, 0)


def shards(*arrays):
    array = pl.BlockSpec(memory_space=pl.ANY)
    whole = pltpu.VMEM((POS, WIDTH), jnp.bfloat16)
    dma = pltpu.SemaphoreType.DMA
    products = 12 * 2 * HEADS * POS * POS * HEAD_DIM
    grads = pl.pallas_call(
        kernel,
        out_shape=[jax.ShapeDtypeStruct((POS, WIDTH), jnp.bfloat16)] * 5,
        in_specs=[array] * 6,
        out_specs=[array] * 5,
        scratch_shapes=[
            whole, whole, whole, whole, whole,
            pltpu.VMEM((4, POS, WIDTH), jnp.bfloat16),
            pltpu.VMEM((3, POS, WIDTH), jnp.bfloat16),
            pltpu.VMEM((3, POS, WIDTH), jnp.bfloat16),
            pltpu.VMEM((OWN, POS), jnp.float32),
            dma((3, CHUNKS)), dma((7,)), dma((3, CHUNKS)), dma((CHUNKS,)), dma((CHUNKS,)),
            dma((2,)), dma((1,)), dma((3, CHUNKS)),
        ],
        compiler_params=pltpu.CompilerParams(has_side_effects=True, vmem_limit_bytes=60 << 20),
        cost_estimate=pl.CostEstimate(
            flops=products,
            bytes_accessed=22 * POS * WIDTH,
            transcendentals=3 * HEADS * POS * POS,
        ),
        name="attention",
    )(*(array.reshape(POS, WIDTH) for array in arrays))
    return tuple(entry[None] for entry in grads)


def solution(mesh):
    spec = P(("dp", "seq"), None, None)
    return jax.shard_map(
        shards, mesh=mesh, in_specs=(spec,) * 6, out_specs=(spec,) * 5, check_vma=False
    )
```

time: 404 us -> 196 us (0.49); the launches traced: 396 us -> 196 us
  Pallas kernels: 0 us -> 183 us
  local copies, waits for them, and re-layouts: 188 us -> 11.7 us
  other arithmetic: 82.1 us -> 0 us
  matrix products: 64 us -> 0 us
  starting transfers between devices: 58.7 us -> 0 us
    pallas_call x0 -> x1, Pallas kernels: none -> 183 us  [shards(): pl.pallas_call(kernel, out_shape=[jax.ShapeDtypeStruct((POS, WIDTH), jnp....]
    unnamed x54 -> x13, local copies, waits for them, and re-layouts: 103 us -> 11.7 us
    all_to_all x7 -> x0, starting transfers between devices: 58.7 us -> none  [the longest x1 9.01 us: shards(): lax.all_to_all(grad_out, 'seq', split_axis=1, concat_axis=0, tiled=True)]
    unnamed x4 -> x0, other arithmetic: 56.2 us -> none
    dot_general x10 -> x0, matrix products: 53.9 us -> none  [product(): return jnp.einsum(form, left, right, preferred_element_type=jnp.float32)]
    all_to_all x4 -> x0, local copies, waits for them, and re-layouts: 51.4 us -> none  [the longest x1 12.9 us: shards(): lax.all_to_all(space_out, 'seq', split_axis=1, concat_axis=0, tiled=True)]
    reshape x7 -> x0, local copies, waits for them, and re-layouts: 28.1 us -> none  [the longest x3 11.4 us: space_major(): tensor.reshape(tensor.shape[:-1] + (HEADS, HEAD_DIM)).transpose(0, 2, 1, 3)]
    convert_element_type x2 -> x0, other arithmetic: 16.5 us -> none  [attend_backward(): score_grads = score_grads.astype(jnp.bfloat16)]
  transfers between devices with their start and end apart: 7 -> 0, of which waited for: 1 -> 0; matrix products, arithmetic and copies ran while one was open for 74% -> 0% of each run, Pallas kernels for 0% -> 0%
where the time goes in v1:
time: 196 us
  Pallas kernels  183 us (93%)
  local copies, waits for them, and re-layouts  11.7 us (6%)
    pallas_call x1, Pallas kernels, shards(): pl.pallas_call(kernel, out_shape=[jax.ShapeDtypeStruct((POS, WIDTH), jnp....  183 us
    unnamed x13, local copies, waits for them, and re-layouts  11.7 us

profile of v1, /device:TPU:0, one launch (start us, length us, event | category | flops | bytes accessed | tf_op | source)
XLA Modules:
  0.0 195.5 jit_solution(17810734343814187540)
XLA Ops:
  0.6 183.2 %attention.1 = (bf16[512,2048]{1,0:T(8,128)(2,1)}, bf16[512,2048]{1,0:T(8,128)(2,1)}, bf16[512,2048]{1,0:T(8,128)(2,1)}, bf16[512,2048]{1,0:T(8,128)(2,1)}, bf16[512,2048]{1,0:T(8,128)(2,1)}) custom-call(bf16[512,2048]{1,0:T(8,128)(2,1)} %bitcast.16, bf16[512,2048]{1,0:T(8,128)(2,1)} %bitcast.17, bf16[512,2048]{1,0:T(8,128)(2,1)} %bitcast.18, ...), custom_call_target="tpu_custom_call" | custom-call | flops 12884901888 | bytes 23068672 | tf_op jit(solution)/shard_map/attention/pallas_call | solution.py:226
  183.8 0.0 copy-start.3
  183.8 3.3 %copy.16 = bf16[1,512,2048]{2,1,0:T(8,128)(2,1)} copy(bf16[1,512,2048]{2,1,0:T(8,128)(2,1)} %bitcast.15) | data formatting | bytes 4194304
  187.1 0.0 copy-done.3
  187.1 0.0 copy-start.2
  187.1 1.3 copy.17
  188.5 1.0 copy-done.2
  189.5 0.0 copy-start.1
  189.5 1.3 copy.18
  190.8 1.0 copy-done.1
  191.8 0.0 copy-start
  191.8 1.3 copy.19
  193.2 1.0 copy-done
  194.2 1.3 copy.20
Async XLA Ops:
  183.8 3.3 %copy-start.3 = (bf16[512,2048]{1,0:T(8,128)(2,1)S(1)}, bf16[512,2048]{1,0:T(8,128)(2,1)}, u32[]{:S(2)}) copy-start(bf16[512,2048]{1,0:T(8,128)(2,1)} %get-tuple-element.11) | copy-start | bytes 6291460
  187.1 2.3 %copy-start.2 = (bf16[512,2048]{1,0:T(8,128)(2,1)S(1)}, bf16[512,2048]{1,0:T(8,128)(2,1)}, u32[]{:S(2)}) copy-start(bf16[512,2048]{1,0:T(8,128)(2,1)} %get-tuple-element.12) | copy-start | bytes 6291460
  189.5 2.3 %copy-start.1 = (bf16[512,2048]{1,0:T(8,128)(2,1)S(1)}, bf16[512,2048]{1,0:T(8,128)(2,1)}, u32[]{:S(2)}) copy-start(bf16[512,2048]{1,0:T(8,128)(2,1)} %get-tuple-element.13) | copy-start | bytes 6291460
  191.8 2.3 %copy-start = (bf16[512,2048]{1,0:T(8,128)(2,1)S(1)}, bf16[512,2048]{1,0:T(8,128)(2,1)}, u32[]{:S(2)}) copy-start(bf16[512,2048]{1,0:T(8,128)(2,1)} %get-tuple-element.14) | copy-start | bytes 6291460

commit v2 on v1

--- a/solution.py
+++ b/solution.py
@@ -43,27 +43,25 @@
     return scores * (1.0 / jnp.sum(scores, axis=0, keepdims=True))
 
 
-def backward(queries, key_rows, values, upstream, bias=None):
-    weights = probabilities(queries, key_rows, bias)
-    value_grads = plain(weights.astype(jnp.bfloat16), upstream)
+def score_backward(queries, key_rows, values, weights, upstream):
     weight_grads = against(values, upstream)
     weighted = weights * weight_grads
     score_grads = weighted - weights * jnp.sum(weighted, axis=0, keepdims=True)
     score_grads = score_grads.astype(jnp.bfloat16)
     key_grads = plain(score_grads, queries) * SCALE
     query_grads = (plain(key_rows.T, score_grads) * SCALE).T
-    return (
-        query_grads.astype(jnp.bfloat16),
-        key_grads.astype(jnp.bfloat16),
-        value_grads.astype(jnp.bfloat16),
-    )
+    return query_grads.astype(jnp.bfloat16), key_grads.astype(jnp.bfloat16)
+
+
+def value_backward(weights, upstream):
+    return plain(weights.astype(jnp.bfloat16), upstream).astype(jnp.bfloat16)
 
 
 def kernel(
     q_space, k_space, v_space, q_time, k_time, grad_out,
     gq_space, gk_space, gv_space, gq_time, gk_time,
-    sq, sk, sv, so, gs, held, made, done, bias,
-    load_sem, send_sem, qkg_sem, so_sem, gs_sem, back_sem, own_sem, store_sem,
+    sq, sk, sv, so, gs, held, made, bias,
+    load_sem, send_sem, qkg_sem, so_sem, gs_sem, back_sem,
 ):
     seq, dp = lax.axis_index("seq"), lax.axis_index("dp")
     my_rows = pl.ds(pl.multiple_of(seq * OWN, OWN), OWN)
@@ -149,24 +147,39 @@
 
     lax.fori_loop(0, CHUNKS, space_forward, 0)
 
-    def time_core(chunk, carry):
+    def each_head(chunk, work):
+        def one(index, carry):
+            work(head_columns(chunk * CHUNK_HEADS + index))
+            return carry
+
+        lax.fori_loop(0, CHUNK_HEADS, one, 0)
+
+    def time_weights(here):
+        return probabilities(held[0, :, here], held[1, :, here], bias[...])
+
+    def time_values(chunk, carry):
         cols = columns(chunk)
         for at in range(3):
             wait_for(held.at[at, :, cols], qkg_sem.at[at, chunk])
-        wait_for(held.at[3, :, cols], so_sem.at[chunk])
-
-        def one(index, carry):
-            here = head_columns(chunk * CHUNK_HEADS + index)
-            query_grads, key_grads, value_grads = backward(
-                held[0, :, here], held[1, :, here], held[3, :, here], held[2, :, here], bias[...]
+
+        def work(here):
+            made[0, :, here] = value_backward(time_weights(here), held[2, :, here])
+
+        each_head(chunk, work)
+        spread(chunk, [(made.at[0], gs, send_sem.at[4], gs_sem.at[chunk])])
+        return carry
+
+    lax.fori_loop(0, CHUNKS, time_values, 0)
+
+    def time_scores(chunk, carry):
+        wait_for(held.at[3, :, columns(chunk)], so_sem.at[chunk])
+
+        def work(here):
+            made[1, :, here], made[2, :, here] = score_backward(
+                held[0, :, here], held[1, :, here], held[3, :, here], time_weights(here), held[2, :, here]
             )
-            made[0, :, here] = value_grads
-            made[1, :, here] = query_grads
-            made[2, :, here] = key_grads
-            return carry
-
-        lax.fori_loop(0, CHUNK_HEADS, one, 0)
-        spread(chunk, [(made.at[0], gs, send_sem.at[4], gs_sem.at[chunk])])
+
+        each_head(chunk, work)
         spread(
             chunk,
             [
@@ -176,26 +189,19 @@
         )
         return carry
 
-    lax.fori_loop(0, CHUNKS, time_core, 0)
-
-    outs = (gq_space, gk_space, gv_space)
+    lax.fori_loop(0, CHUNKS, time_scores, 0)
 
     def space_back(chunk, carry):
-        cols = columns(chunk)
-        wait_for(gs.at[:, cols], gs_sem.at[chunk])
-
-        def one(index, carry):
-            here = head_columns(chunk * CHUNK_HEADS + index)
-            grads = backward(sq[:, here], sk[:, here], sv[:, here], gs[:, here])
-            for at in range(3):
-                done[at, :, here] = grads[at]
-            return carry
-
-        lax.fori_loop(0, CHUNK_HEADS, one, 0)
-        for at in range(3):
-            pltpu.make_async_copy(
-                done.at[at, :, cols], outs[at].at[:, cols], store_sem.at[at, chunk]
-            ).start()
+        wait_for(gs.at[:, columns(chunk)], gs_sem.at[chunk])
+
+        def work(here):
+            weights = probabilities(sq[:, here], sk[:, here])
+            gv_space[:, here] = value_backward(weights, gs[:, here])
+            gq_space[:, here], gk_space[:, here] = score_backward(
+                sq[:, here], sk[:, here], sv[:, here], weights, gs[:, here]
+            )
+
+        each_head(chunk, work)
         return carry
 
     lax.fori_loop(0, CHUNKS, space_back, 0)
@@ -206,16 +212,17 @@
     wait_for(gq_time, back_sem.at[0])
     wait_for(gk_time, back_sem.at[1])
 
-    def stored(chunk, carry):
-        for at in range(3):
-            pltpu.make_async_copy(
-                done.at[at, :, columns(chunk)],
-                outs[at].at[:, columns(chunk)],
-                store_sem.at[at, chunk],
-            ).wait()
-        return carry
-
-    lax.fori_loop(0, CHUNKS, stored, 0)
+
+def write_out(*refs):
+    sources, targets, sem = refs[:5], refs[5:10], refs[10]
+    copies = [
+        pltpu.make_async_copy(source, target, sem.at[at])
+        for at, (source, target) in enumerate(zip(sources, targets))
+    ]
+    for copy in copies:
+        copy.start()
+    for copy in copies:
+        copy.wait()
 
 
 def shards(*arrays):
@@ -225,26 +232,36 @@
     products = 12 * 2 * HEADS * POS * POS * HEAD_DIM
     grads = pl.pallas_call(
         kernel,
-        out_shape=[jax.ShapeDtypeStruct((POS, WIDTH), jnp.bfloat16)] * 5,
+        out_shape=[pltpu.VMEM((POS, WIDTH), jnp.bfloat16)] * 5,
         in_specs=[array] * 6,
-        out_specs=[array] * 5,
+        out_specs=[pl.BlockSpec(memory_space=pltpu.VMEM)] * 5,
         scratch_shapes=[
             whole, whole, whole, whole, whole,
             pltpu.VMEM((4, POS, WIDTH), jnp.bfloat16),
             pltpu.VMEM((3, POS, WIDTH), jnp.bfloat16),
-            pltpu.VMEM((3, POS, WIDTH), jnp.bfloat16),
             pltpu.VMEM((OWN, POS), jnp.float32),
-            dma((3, CHUNKS)), dma((7,)), dma((3, CHUNKS)), dma((CHUNKS,)), dma((CHUNKS,)),
-            dma((2,)), dma((1,)), dma((3, CHUNKS)),
+            dma((3, CHUNKS)), dma((7,)), dma((3, CHUNKS)), dma((CHUNKS,)), dma((CHUNKS,)), dma((2,)),
         ],
-        compiler_params=pltpu.CompilerParams(has_side_effects=True, vmem_limit_bytes=60 << 20),
+        compiler_params=pltpu.CompilerParams(has_side_effects=True, vmem_limit_bytes=46 << 20),
         cost_estimate=pl.CostEstimate(
             flops=products,
-            bytes_accessed=22 * POS * WIDTH,
-            transcendentals=3 * HEADS * POS * POS,
+            bytes_accessed=12 * POS * WIDTH,
+            transcendentals=4 * HEADS * POS * POS,
         ),
         name="attention",
     )(*(array.reshape(POS, WIDTH) for array in arrays))
+    grads = pl.pallas_call(
+        write_out,
+        out_shape=[jax.ShapeDtypeStruct((POS, WIDTH), jnp.bfloat16)] * 5,
+        in_specs=[array] * 5,
+        out_specs=[array] * 5,
+        scratch_shapes=[dma((5,))],
+        compiler_params=pltpu.CompilerParams(vmem_limit_bytes=1 << 20),
+        cost_estimate=pl.CostEstimate(
+            flops=0, bytes_accessed=20 * POS * WIDTH, transcendentals=0
+        ),
+        name="write_out",
+    )(*grads)
     return tuple(entry[None] for entry in grads)
 
 

time: 196 us -> 188 us (0.959)
  local copies, waits for them, and re-layouts: 11.7 us -> 0 us
  Pallas kernels: 183 us -> 187 us
    unnamed x13 -> x0, local copies, waits for them, and re-layouts: 11.7 us -> none
    pallas_call x1 -> x2, Pallas kernels: 183 us -> 187 us  [the longest x1 183 us: shards(): pl.pallas_call(kernel, out_shape=[pltpu.VMEM((POS, WIDTH), jnp.bfloat16)]...]
where the time goes in v2:
time: 188 us
  Pallas kernels  187 us (99%)
    pallas_call x1, Pallas kernels, shards(): pl.pallas_call(kernel, out_shape=[pltpu.VMEM((POS, WIDTH), jnp.bfloat16)]...  183 us
    pallas_call x1, Pallas kernels, shards(): pl.pallas_call(write_out, out_shape=[jax.ShapeDtypeStruct((POS, WIDTH), j...  4.01 us

profile of v2, /device:TPU:0, one launch (start us, length us, event | category | flops | bytes accessed | tf_op | source)
XLA Modules:
  0.0 187.6 jit_solution(17235105766949558553)
XLA Ops:
  0.6 182.9 %attention.1 = (bf16[512,2048]{1,0:T(8,128)(2,1)S(1)}, bf16[512,2048]{1,0:T(8,128)(2,1)S(1)}, bf16[512,2048]{1,0:T(8,128)(2,1)S(1)}, bf16[512,2048]{1,0:T(8,128)(2,1)S(1)}, bf16[512,2048]{1,0:T(8,128)(2,1)S(1)}) custom-call(bf16[512,2048]{1,0:T(8,128)(2,1)} %bitcast.11, bf16[512,2048]{1,0:T(8,128)(2,1)} %bitcast.12, bf16[512,2048]{1,0:T(8,128)(2,1)} %bitcast.13, ...), custom_call_target="tpu_custom_call" | custom-call | flops 12884901888 | bytes 12582912 | tf_op jit(solution)/shard_map/attention/pallas_call | solution.py:233
  183.6 4.0 %write_out.1 = (bf16[512,2048]{1,0:T(8,128)(2,1)}, bf16[512,2048]{1,0:T(8,128)(2,1)}, bf16[512,2048]{1,0:T(8,128)(2,1)}, bf16[512,2048]{1,0:T(8,128)(2,1)}, bf16[512,2048]{1,0:T(8,128)(2,1)}) custom-call(bf16[512,2048]{1,0:T(8,128)(2,1)S(1)} %get-tuple-element.15.refs_0_, bf16[512,2048]{1,0:T(8,128)(2,1)S(1)} %get-tuple-element.16.refs_1_, ...), custom_call_target="tpu_custom_call" | custom-call | bytes 20971520 | tf_op jit(solution)/shard_map/write_out/pallas_call | solution.py:253

commit v3 on v2

--- a/solution.py
+++ b/solution.py
@@ -18,7 +18,7 @@
 POS = 512
 OWN = POS // FRAMES
 WIDTH = HEADS * HEAD_DIM
-CHUNKS = 4
+CHUNKS = 8
 COLS = WIDTH // CHUNKS
 CHUNK_HEADS = HEADS // CHUNKS
 
@@ -81,27 +81,23 @@
     def rows_of(device):
         return pl.ds(pl.multiple_of(device * OWN, OWN), OWN)
 
-    def spread(chunk, moves):
+    def spread(chunk, source, target, sent, landed):
         cols = columns(chunk)
 
         def one(step, carry):
             peer = peer_of(step)
-            for source, target, sent, landed in moves:
-                pltpu.make_async_remote_copy(
-                    src_ref=source.at[rows_of(peer), cols],
-                    dst_ref=target.at[my_rows, cols],
-                    send_sem=sent,
-                    recv_sem=landed,
-                    device_id=(dp, peer),
-                    device_id_type=MESH,
-                ).start()
+            pltpu.make_async_remote_copy(
+                src_ref=source.at[rows_of(peer), cols],
+                dst_ref=target.at[my_rows, cols],
+                send_sem=sent,
+                recv_sem=landed,
+                device_id=(dp, peer),
+                device_id_type=MESH,
+            ).start()
             return carry
 
         lax.fori_loop(1, FRAMES, one, 0)
-        for source, target, sent, landed in moves:
-            pltpu.make_async_copy(
-                source.at[my_rows, cols], target.at[my_rows, cols], landed
-            ).start()
+        pltpu.make_async_copy(source.at[my_rows, cols], target.at[my_rows, cols], landed).start()
 
     def wait_for(ref, sem):
         pltpu.make_async_copy(ref, ref, sem).wait()
@@ -115,13 +111,8 @@
             ).start()
 
     def send_inputs(chunk, carry):
-        spread(
-            chunk,
-            [
-                (source, held.at[at], send_sem.at[at], qkg_sem.at[at, chunk])
-                for at, source in enumerate((q_time, k_time, grad_out))
-            ],
-        )
+        for at, source in enumerate((q_time, k_time, grad_out)):
+            spread(chunk, source, held.at[at], send_sem.at[at], qkg_sem.at[at, chunk])
         return carry
 
     lax.fori_loop(0, CHUNKS, send_inputs, 0)
@@ -142,7 +133,7 @@
             return carry
 
         lax.fori_loop(0, CHUNK_HEADS, one, 0)
-        spread(chunk, [(so, held.at[3], send_sem.at[3], so_sem.at[chunk])])
+        spread(chunk, so, held.at[3], send_sem.at[3], so_sem.at[chunk])
         return carry
 
     lax.fori_loop(0, CHUNKS, space_forward, 0)
@@ -166,7 +157,7 @@
             made[0, :, here] = value_backward(time_weights(here), held[2, :, here])
 
         each_head(chunk, work)
-        spread(chunk, [(made.at[0], gs, send_sem.at[4], gs_sem.at[chunk])])
+        spread(chunk, made.at[0], gs, send_sem.at[4], gs_sem.at[chunk])
         return carry
 
     lax.fori_loop(0, CHUNKS, time_values, 0)
@@ -180,13 +171,8 @@
             )
 
         each_head(chunk, work)
-        spread(
-            chunk,
-            [
-                (made.at[1], gq_time, send_sem.at[5], back_sem.at[0]),
-                (made.at[2], gk_time, send_sem.at[6], back_sem.at[1]),
-            ],
-        )
+        spread(chunk, made.at[1], gq_time, send_sem.at[5], back_sem.at[0])
+        spread(chunk, made.at[2], gk_time, send_sem.at[6], back_sem.at[1])
         return carry
 
     lax.fori_loop(0, CHUNKS, time_scores, 0)

time: 188 us -> 180 us (0.957)
  Pallas kernels: 187 us -> 179 us
    pallas_call x1, Pallas kernels: 183 us -> 175 us  [shards(): pl.pallas_call(kernel, out_shape=[pltpu.VMEM((POS, WIDTH), jnp.bfloat16)]...]
where the time goes in v3:
time: 180 us
  Pallas kernels  179 us (99%)
    pallas_call x1, Pallas kernels, shards(): pl.pallas_call(kernel, out_shape=[pltpu.VMEM((POS, WIDTH), jnp.bfloat16)]...  175 us
    pallas_call x1, Pallas kernels, shards(): pl.pallas_call(write_out, out_shape=[jax.ShapeDtypeStruct((POS, WIDTH), j...  4.01 us

profile of v3, /device:TPU:0, one launch (start us, length us, event | category | flops | bytes accessed | tf_op | source)
XLA Modules:
  0.0 179.9 jit_solution(13128751111345482559)
XLA Ops:
  0.6 175.3 %attention.1 = (bf16[512,2048]{1,0:T(8,128)(2,1)S(1)}, bf16[512,2048]{1,0:T(8,128)(2,1)S(1)}, bf16[512,2048]{1,0:T(8,128)(2,1)S(1)}, bf16[512,2048]{1,0:T(8,128)(2,1)S(1)}, bf16[512,2048]{1,0:T(8,128)(2,1)S(1)}) custom-call(bf16[512,2048]{1,0:T(8,128)(2,1)} %bitcast.11, bf16[512,2048]{1,0:T(8,128)(2,1)} %bitcast.12, bf16[512,2048]{1,0:T(8,128)(2,1)} %bitcast.13, ...), custom_call_target="tpu_custom_call" | custom-call | flops 12884901888 | bytes 12582912 | tf_op jit(solution)/shard_map/attention/pallas_call | solution.py:219
  175.9 4.0 %write_out.1 = (bf16[512,2048]{1,0:T(8,128)(2,1)}, bf16[512,2048]{1,0:T(8,128)(2,1)}, bf16[512,2048]{1,0:T(8,128)(2,1)}, bf16[512,2048]{1,0:T(8,128)(2,1)}, bf16[512,2048]{1,0:T(8,128)(2,1)}) custom-call(bf16[512,2048]{1,0:T(8,128)(2,1)S(1)} %get-tuple-element.15.refs_0_, bf16[512,2048]{1,0:T(8,128)(2,1)S(1)} %get-tuple-element.16.refs_1_, ...), custom_call_target="tpu_custom_call" | custom-call | bytes 20971520 | tf_op jit(solution)/shard_map/write_out/pallas_call | solution.py:239

commit v4 on v3

--- a/solution.py
+++ b/solution.py
@@ -101,6 +101,15 @@
 
     def wait_for(ref, sem):
         pltpu.make_async_copy(ref, ref, sem).wait()
+
+    barrier = pltpu.get_barrier_semaphore()
+
+    def greet(step, carry):
+        pl.semaphore_signal(barrier, inc=1, device_id=(dp, peer_of(step)), device_id_type=MESH)
+        return carry
+
+    lax.fori_loop(1, FRAMES, greet, 0)
+    pl.semaphore_wait(barrier, FRAMES - 1)
 
     spatial = ((q_space, sq), (k_space, sk), (v_space, sv))
     for chunk in range(CHUNKS):
@@ -228,7 +237,7 @@
             pltpu.VMEM((OWN, POS), jnp.float32),
             dma((3, CHUNKS)), dma((7,)), dma((3, CHUNKS)), dma((CHUNKS,)), dma((CHUNKS,)), dma((2,)),
         ],
-        compiler_params=pltpu.CompilerParams(has_side_effects=True, vmem_limit_bytes=46 << 20),
+        compiler_params=pltpu.CompilerParams(collective_id=0, has_side_effects=True, vmem_limit_bytes=46 << 20),
         cost_estimate=pl.CostEstimate(
             flops=products,
             bytes_accessed=12 * POS * WIDTH,

time: 180 us -> 173 us (0.961)
  Pallas kernels: 179 us -> 172 us
    pallas_call x1, Pallas kernels: 175 us -> 168 us  [shards(): pl.pallas_call(kernel, out_shape=[pltpu.VMEM((POS, WIDTH), jnp.bfloat16)]...]
where the time goes in v4:
time: 173 us
  Pallas kernels  172 us (99%)
    pallas_call x1, Pallas kernels, shards(): pl.pallas_call(kernel, out_shape=[pltpu.VMEM((POS, WIDTH), jnp.bfloat16)]...  168 us
    pallas_call x1, Pallas kernels, shards(): pl.pallas_call(write_out, out_shape=[jax.ShapeDtypeStruct((POS, WIDTH), j...  4.01 us

profile of v4, /device:TPU:0, one launch (start us, length us, event | category | flops | bytes accessed | tf_op | source)
XLA Modules:
  0.0 172.9 jit_solution(7717732515630253140)
XLA Ops:
  0.6 168.3 %attention.1 = (bf16[512,2048]{1,0:T(8,128)(2,1)S(1)}, bf16[512,2048]{1,0:T(8,128)(2,1)S(1)}, bf16[512,2048]{1,0:T(8,128)(2,1)S(1)}, bf16[512,2048]{1,0:T(8,128)(2,1)S(1)}, bf16[512,2048]{1,0:T(8,128)(2,1)S(1)}) custom-call(bf16[512,2048]{1,0:T(8,128)(2,1)} %bitcast.11, bf16[512,2048]{1,0:T(8,128)(2,1)} %bitcast.12, bf16[512,2048]{1,0:T(8,128)(2,1)} %bitcast.13, ...), custom_call_target="tpu_custom_call" | custom-call | flops 12884901888 | bytes 12582912 | tf_op jit(solution)/shard_map/attention/pallas_call | solution.py:228
  168.9 4.0 %write_out.1 = (bf16[512,2048]{1,0:T(8,128)(2,1)}, bf16[512,2048]{1,0:T(8,128)(2,1)}, bf16[512,2048]{1,0:T(8,128)(2,1)}, bf16[512,2048]{1,0:T(8,128)(2,1)}, bf16[512,2048]{1,0:T(8,128)(2,1)}) custom-call(bf16[512,2048]{1,0:T(8,128)(2,1)S(1)} %get-tuple-element.15.refs_0_, bf16[512,2048]{1,0:T(8,128)(2,1)S(1)} %get-tuple-element.16.refs_1_, ...), custom_call_target="tpu_custom_call" | custom-call | bytes 20971520 | tf_op jit(solution)/shard_map/write_out/pallas_call | solution.py:248

commit v5 on v4

--- a/solution.py
+++ b/solution.py
@@ -104,13 +104,8 @@
 
     barrier = pltpu.get_barrier_semaphore()
 
-    def greet(step, carry):
+    for step in range(1, FRAMES):
         pl.semaphore_signal(barrier, inc=1, device_id=(dp, peer_of(step)), device_id_type=MESH)
-        return carry
-
-    lax.fori_loop(1, FRAMES, greet, 0)
-    pl.semaphore_wait(barrier, FRAMES - 1)
-
     spatial = ((q_space, sq), (k_space, sk), (v_space, sv))
     for chunk in range(CHUNKS):
         cols = pl.ds(chunk * COLS, COLS)
@@ -118,6 +113,8 @@
             pltpu.make_async_copy(
                 source.at[:, cols], target.at[:, cols], load_sem.at[at, chunk]
             ).start()
+
+    pl.semaphore_wait(barrier, FRAMES - 1)
 
     def send_inputs(chunk, carry):
         for at, source in enumerate((q_time, k_time, grad_out)):

time: 173 us -> 172 us (level)
  no operation moved by 1% of the time
where the time goes in v5:
time: 172 us
  Pallas kernels  172 us (100%)
    pallas_call x1, Pallas kernels, shards(): pl.pallas_call(kernel, out_shape=[pltpu.VMEM((POS, WIDTH), jnp.bfloat16)]...  168 us
    pallas_call x1, Pallas kernels, shards(): pl.pallas_call(write_out, out_shape=[jax.ShapeDtypeStruct((POS, WIDTH), j...  4.01 us

profile of v5, /device:TPU:0, one launch (start us, length us, event | category | flops | bytes accessed | tf_op | source)
XLA Modules:
  0.0 172.3 jit_solution(9159747624837412760)
XLA Ops:
  0.6 167.6 %attention.1 = (bf16[512,2048]{1,0:T(8,128)(2,1)S(1)}, bf16[512,2048]{1,0:T(8,128)(2,1)S(1)}, bf16[512,2048]{1,0:T(8,128)(2,1)S(1)}, bf16[512,2048]{1,0:T(8,128)(2,1)S(1)}, bf16[512,2048]{1,0:T(8,128)(2,1)S(1)}) custom-call(bf16[512,2048]{1,0:T(8,128)(2,1)} %bitcast.11, bf16[512,2048]{1,0:T(8,128)(2,1)} %bitcast.12, bf16[512,2048]{1,0:T(8,128)(2,1)} %bitcast.13, ...), custom_call_target="tpu_custom_call" | custom-call | flops 12884901888 | bytes 12582912 | tf_op jit(solution)/shard_map/attention/pallas_call | solution.py:225
  168.3 4.0 %write_out.1 = (bf16[512,2048]{1,0:T(8,128)(2,1)}, bf16[512,2048]{1,0:T(8,128)(2,1)}, bf16[512,2048]{1,0:T(8,128)(2,1)}, bf16[512,2048]{1,0:T(8,128)(2,1)}, bf16[512,2048]{1,0:T(8,128)(2,1)}) custom-call(bf16[512,2048]{1,0:T(8,128)(2,1)S(1)} %get-tuple-element.15.refs_0_, bf16[512,2048]{1,0:T(8,128)(2,1)S(1)} %get-tuple-element.16.refs_1_, ...), custom_call_target="tpu_custom_call" | custom-call | bytes 20971520 | tf_op jit(solution)/shard_map/write_out/pallas_call | solution.py:245

commit v6 on v5

--- a/solution.py
+++ b/solution.py
@@ -18,7 +18,7 @@
 POS = 512
 OWN = POS // FRAMES
 WIDTH = HEADS * HEAD_DIM
-CHUNKS = 8
+CHUNKS = 4
 COLS = WIDTH // CHUNKS
 CHUNK_HEADS = HEADS // CHUNKS
 
@@ -116,18 +116,16 @@
 
     pl.semaphore_wait(barrier, FRAMES - 1)
 
-    def send_inputs(chunk, carry):
+    def send_inputs(chunk):
         for at, source in enumerate((q_time, k_time, grad_out)):
             spread(chunk, source, held.at[at], send_sem.at[at], qkg_sem.at[at, chunk])
-        return carry
-
-    lax.fori_loop(0, CHUNKS, send_inputs, 0)
 
     rows = lax.broadcasted_iota(jnp.int32, (OWN, POS), 0)
     lanes = lax.broadcasted_iota(jnp.int32, (OWN, POS), 1)
     bias[...] = jnp.where(rows == lanes % OWN, 0.0, -1e30).astype(jnp.float32)
 
     def space_forward(chunk, carry):
+        send_inputs(chunk)
         cols = columns(chunk)
         for at, (source, target) in enumerate(spatial):
             wait_for(target.at[:, cols], load_sem.at[at, chunk])

time: 172 us -> 172 us (level)
  no operation moved by 1% of the time
where the time goes in v6:
time: 172 us
  Pallas kernels  172 us (100%)
    pallas_call x1, Pallas kernels, shards(): pl.pallas_call(kernel, out_shape=[pltpu.VMEM((POS, WIDTH), jnp.bfloat16)]...  168 us
    pallas_call x1, Pallas kernels, shards(): pl.pallas_call(write_out, out_shape=[jax.ShapeDtypeStruct((POS, WIDTH), j...  4.01 us

profile of v6, /device:TPU:0, one launch (start us, length us, event | category | flops | bytes accessed | tf_op | source)
XLA Modules:
  0.0 172.3 jit_solution(13864126739946552745)
XLA Ops:
  0.6 167.7 %attention.1 = (bf16[512,2048]{1,0:T(8,128)(2,1)S(1)}, bf16[512,2048]{1,0:T(8,128)(2,1)S(1)}, bf16[512,2048]{1,0:T(8,128)(2,1)S(1)}, bf16[512,2048]{1,0:T(8,128)(2,1)S(1)}, bf16[512,2048]{1,0:T(8,128)(2,1)S(1)}) custom-call(bf16[512,2048]{1,0:T(8,128)(2,1)} %bitcast.11, bf16[512,2048]{1,0:T(8,128)(2,1)} %bitcast.12, bf16[512,2048]{1,0:T(8,128)(2,1)} %bitcast.13, ...), custom_call_target="tpu_custom_call" | custom-call | flops 12884901888 | bytes 12582912 | tf_op jit(solution)/shard_map/attention/pallas_call | solution.py:223
  168.3 4.0 %write_out.1 = (bf16[512,2048]{1,0:T(8,128)(2,1)}, bf16[512,2048]{1,0:T(8,128)(2,1)}, bf16[512,2048]{1,0:T(8,128)(2,1)}, bf16[512,2048]{1,0:T(8,128)(2,1)}, bf16[512,2048]{1,0:T(8,128)(2,1)}) custom-call(bf16[512,2048]{1,0:T(8,128)(2,1)S(1)} %get-tuple-element.15.refs_0_, bf16[512,2048]{1,0:T(8,128)(2,1)S(1)} %get-tuple-element.16.refs_1_, ...), custom_call_target="tpu_custom_call" | custom-call | bytes 20971520 | tf_op jit(solution)/shard_map/write_out/pallas_call | solution.py:243

commit v7 on v6

--- a/solution.py
+++ b/solution.py
@@ -85,7 +85,7 @@
         cols = columns(chunk)
 
         def one(step, carry):
-            peer = peer_of(step)
+            peer = peer_of(lax.rem(step * 11, FRAMES))
             pltpu.make_async_remote_copy(
                 src_ref=source.at[rows_of(peer), cols],
                 dst_ref=target.at[my_rows, cols],

time: 172 us -> 172 us (level)
  no operation moved by 1% of the time
where the time goes in v7:
time: 172 us
  Pallas kernels  172 us (100%)
    pallas_call x1, Pallas kernels, shards(): pl.pallas_call(kernel, out_shape=[pltpu.VMEM((POS, WIDTH), jnp.bfloat16)]...  168 us
    pallas_call x1, Pallas kernels, shards(): pl.pallas_call(write_out, out_shape=[jax.ShapeDtypeStruct((POS, WIDTH), j...  4.01 us

profile of v7, /device:TPU:0, one launch (start us, length us, event | category | flops | bytes accessed | tf_op | source)
XLA Modules:
  0.0 172.3 jit_solution(3221579528308826772)
XLA Ops:
  0.6 167.6 %attention.1 = (bf16[512,2048]{1,0:T(8,128)(2,1)S(1)}, bf16[512,2048]{1,0:T(8,128)(2,1)S(1)}, bf16[512,2048]{1,0:T(8,128)(2,1)S(1)}, bf16[512,2048]{1,0:T(8,128)(2,1)S(1)}, bf16[512,2048]{1,0:T(8,128)(2,1)S(1)}) custom-call(bf16[512,2048]{1,0:T(8,128)(2,1)} %bitcast.11, bf16[512,2048]{1,0:T(8,128)(2,1)} %bitcast.12, bf16[512,2048]{1,0:T(8,128)(2,1)} %bitcast.13, ...), custom_call_target="tpu_custom_call" | custom-call | flops 12884901888 | bytes 12582912 | tf_op jit(solution)/shard_map/attention/pallas_call | solution.py:223
  168.2 4.0 %write_out.1 = (bf16[512,2048]{1,0:T(8,128)(2,1)}, bf16[512,2048]{1,0:T(8,128)(2,1)}, bf16[512,2048]{1,0:T(8,128)(2,1)}, bf16[512,2048]{1,0:T(8,128)(2,1)}, bf16[512,2048]{1,0:T(8,128)(2,1)}) custom-call(bf16[512,2048]{1,0:T(8,128)(2,1)S(1)} %get-tuple-element.15.refs_0_, bf16[512,2048]{1,0:T(8,128)(2,1)S(1)} %get-tuple-element.16.refs_1_, ...), custom_call_target="tpu_custom_call" | custom-call | bytes 20971520 | tf_op jit(solution)/shard_map/write_out/pallas_call | solution.py:243
